TPU v7x, 32 devices: a whole 2x2x4 slice. The times are simulated.
32 devices in a mesh: dp: 8 (over y, x, core), tensor: 4 (over z).
Axes of the slice: x: 2, y: 2, z: 4, core: 2. Of those that a mesh axis runs over, the one named last changes fastest.
Arguments:
- points: bfloat16 [8192, 256], P('dp'), as said below
- centers: bfloat16 [32768, 256], P(('dp', 'tensor')), as said below
- factors: bfloat16 [32768, 32768], P('tensor', 'dp'), may hold values from -0.015625 to 0.015625
- column_scale: float32 [32768], P(('dp', 'tensor')), may hold values from 80 to 320
- iterate: float32 [64, 32768], P(None, ('dp', 'tensor')), may hold values from -6 to 6
- residual: float32 [64, 32768], P(None, ('dp', 'tensor')), may hold values from -6 to 6
- direction: float32 [64, 32768], P(None, ('dp', 'tensor')), may hold values from -6 to 6
Outputs:
- new_iterate: float32 [64, 32768], P(None, ('dp', 'tensor'))
- new_residual: float32 [64, 32768], P(None, ('dp', 'tensor'))
- new_direction: float32 [64, 32768], P(None, ('dp', 'tensor'))
Inputs may be any that keep to these rules, and one draw needn't show every extreme that they name: `points`: real embeddings of any row scale. `centers`: real embeddings of any row scale.
All inputs are finite; a program needn't handle non-finite values.
Results may differ from a plain program's by a relative error of at most 0.0058.
The roundings to bfloat16 on the way count: a program that leaves them out, or rounds other values in their place, can miss the bound.
Values may be sent and summed in bfloat16 or wider, within the bound.
A program may use at most 448 MiB of HBM per device.

v0:
```python
import jax
import jax.numpy as jnp
from jax import lax
from jax.sharding import PartitionSpec as P

kernel_gamma = 8.0
ridge_penalty = 0.0001


def normalized(rows):
    widened = rows.astype(jnp.float32)
    inv_rms = lax.rsqrt(jnp.mean(widened * widened, axis=1, keepdims=True) + 1e-06)
    return (widened * inv_rms).astype(jnp.bfloat16)


def rows_in(vector_b):
    return lax.all_gather(vector_b, "dp", axis=1, tiled=True)


def cols_out(partial_value):
    return lax.psum_scatter(partial_value, "tensor", scatter_dimension=1, tiled=True)


def cols_in(vector_b):
    return lax.all_gather(vector_b, "tensor", axis=1, tiled=True)


def rows_out(partial_value):
    return lax.psum_scatter(partial_value, "dp", scatter_dimension=1, tiled=True)


def times_block(vector_rows, block):
    return jnp.dot(vector_rows, block, preferred_element_type=jnp.float32)


def times_block_t(vector_cols, block):
    return lax.dot_general(
        vector_cols, block, (((1,), (1,)), ((), ())), preferred_element_type=jnp.float32
    )


def shards(points, centers, factors, column_scale, iterate, residual, direction):
    piece_len = iterate.shape[1]
    local_rows, local_cols = factors.shape
    dp_index = lax.axis_index("dp")
    tensor_index = lax.axis_index("tensor")
    tensor_count = lax.axis_size("tensor")
    total_points = points.shape[0] * lax.axis_size("dp")
    row_pos = lax.broadcasted_iota(jnp.int32, (local_rows, local_cols), 0)
    row_ids = (row_pos // piece_len * tensor_count + tensor_index) * piece_len + row_pos % piece_len
    col_ids = dp_index * local_cols + lax.broadcasted_iota(jnp.int32, (local_rows, local_cols), 1)
    zero_block = jnp.zeros_like(factors)
    lower = jnp.where(col_ids < row_ids, factors, zero_block)
    upper = jnp.where(col_ids >= row_ids, factors, zero_block)
    scale_row = column_scale[None, :]
    first = scale_row * (
        direction + cols_out(times_block(rows_in(direction.astype(jnp.bfloat16)), lower))
    )
    second = first + rows_out(times_block_t(cols_in(first.astype(jnp.bfloat16)), upper))
    second_rows = rows_in(second.astype(jnp.bfloat16))
    center_rows = lax.all_gather(normalized(centers), "dp", axis=0, tiled=True)
    inner = jnp.dot(normalized(points), center_rows.T, preferred_element_type=jnp.float32)
    kernel = jnp.exp(kernel_gamma * (inner / points.shape[1] - 1.0)).astype(jnp.bfloat16)
    point_part = times_block_t(second_rows, kernel)
    point_vals = lax.psum(point_part, "tensor")
    center_part = times_block(point_vals.astype(jnp.bfloat16), kernel) / total_points
    back = rows_out(center_part)
    back_b_rows = rows_in(back.astype(jnp.bfloat16))
    third = back + cols_out(times_block(back_b_rows, upper)) + ridge_penalty * first
    weighted = scale_row * third
    image = weighted + rows_out(times_block_t(cols_in(weighted.astype(jnp.bfloat16)), lower))
    old_norm, curvature, cross, image_norm = lax.psum(
        (
            jnp.sum(residual * residual, axis=1, keepdims=True),
            jnp.sum(direction * image, axis=1, keepdims=True),
            jnp.sum(residual * image, axis=1, keepdims=True),
            jnp.sum(image * image, axis=1, keepdims=True),
        ),
        ("dp", "tensor"),
    )
    step_size = old_norm / curvature
    new_iterate = iterate + step_size * direction
    new_residual = residual - step_size * image
    new_norm = old_norm - 2.0 * step_size * cross + step_size * step_size * image_norm
    new_direction = new_residual + new_norm / old_norm * direction
    return (new_iterate, new_residual, new_direction)


def solution(mesh):
    return jax.shard_map(
        shards,
        mesh=mesh,
        in_specs=(
            P("dp", None),
            P(("dp", "tensor"), None),
            P("tensor", "dp"),
            P(("dp", "tensor")),
            P(None, ("dp", "tensor")),
            P(None, ("dp", "tensor")),
            P(None, ("dp", "tensor")),
        ),
        out_specs=(P(None, ("dp", "tensor")), P(None, ("dp", "tensor")), P(None, ("dp", "tensor"))),
        check_vma=False,
    )
```

profile of v0, /device:TPU:0, one launch (start us, length us, event | category | flops | bytes accessed | tf_op | source)
XLA Modules:
  0.0 581.6 jit_solution(7413079724310796807)
XLA Ops:
  7.2 0.0 all-gather.5.cloned.1.call-start
  7.2 1.6 convert_element_type.33
  8.8 0.0 all-gather.5.cloned.1.call-update
  8.9 0.0 reduce-scatter.6.cloned.1.call-start
  9.0 66.1 %fusion.3 = (bf16[8192,4096]{1,0:T(8,128)(2,1)}, bf16[8192,4096]{1,0:T(8,128)(2,1)}) fusion(bf16[8192,4096]{1,0:T(8,128)(2,1)} %param.9, s32[8192]{0:T(1024)S(1)} %get-tuple-element.24, s32[8192]{0:T(1024)S(1)} %get-tuple-element.25, s32[]{:T(128)S(6)} %axis_index.25, s32[8192]{0:T(1024)S(1)} %get-tuple-element.23, s32[8192]{0:T(1024)S(1)} %get-tuple-element.26, ...), kind=kLoop, calls=%fused_computation.4 | loop fusion | flops 335544320 | bytes 201490432 | tf_op jit(solution)/shard_map/jit(_where)/select_n | solution.py:54
  75.1 0.0 copy-start
  75.1 0.0 copy-start.6
  75.1 0.0 all-gather.5.cloned.1.call-done
  75.1 0.0 copy-start.1
  75.1 0.0 copy-start.4
  75.1 25.9 %convolution_bitcast_fusion = f32[64,4096]{1,0:T(8,128)} fusion(bf16[64,8192]{1,0:T(8,128)(2,1)} %all-gather.5.cloned.1.call-done, bf16[8192,4096]{1,0:T(8,128)(2,1)} %get-tuple-element.21), kind=kOutput, calls=%fused_computation.7 | convolution fusion | flops 4294967296 | bytes 69206016 | tf_op jit(solution)/shard_map/dot_general | solution.py:33
  101.0 0.0 reduce-scatter.6.cloned.1.call-update
  101.0 0.0 reduce-scatter.8.cloned.1.call-start
  101.1 29.9 %reduce-scatter.6.cloned.1.call-done = f32[64,1024]{1,0:T(8,128)} async-done(((f32[64,4096]{1,0:T(8,128)}), f32[64,1024]{1,0:T(8,128)}) %reduce-scatter.6.cloned.1.call-update) | async-done | bytes 262160 | tf_op jit(solution)/shard_map/reduce_scatter | solution.py:21
  131.0 0.0 copy-done
  131.0 0.0 copy-done.6
  131.0 1.0 fusion.19
  132.0 16.0 %all_gather.19 = bf16[64,4096]{1,0:T(8,128)(2,1)S(1)} all-gather(bf16[64,1024]{1,0:T(8,128)(2,1)S(1)} %get-tuple-element.18), channel_id=1, replica_groups=mesh['dp'=8,'tensor'=4] {'tensor'}, dimensions={1}, use_global_device_ids=true | all-gather | bytes 655360 | tf_op jit(solution)/shard_map/all_gather | solution.py:25
  148.0 30.2 %fusion.20 = f32[64,8192]{1,0:T(8,128)} fusion(bf16[64,4096]{1,0:T(8,128)(2,1)S(1)} %all_gather.19, bf16[8192,4096]{1,0:T(8,128)(2,1)} %get-tuple-element.20), kind=kOutput, calls=%fused_computation.45 | convolution fusion | flops 4294967296 | bytes 69730304 | tf_op jit(solution)/shard_map/dot_general | solution.py:37
  178.2 0.0 reduce-scatter.8.cloned.1.call-update
  178.2 0.0 all-gather.9.cloned.1.call-start
  178.3 0.0 copy-done.1
  178.3 0.2 fusion.6
  178.5 1.0 fusion.7
  179.5 0.0 all-gather.9.cloned.1.call-update
  179.5 0.0 all-gather.7.cloned.1.call-start
  179.6 38.4 %reduce-scatter.8.cloned.1.call-done = f32[64,1024]{1,0:T(8,128)} async-done(((f32[64,8192]{1,0:T(8,128)}), f32[64,1024]{1,0:T(8,128)}) %reduce-scatter.8.cloned.1.call-update) | async-done | bytes 262160 | tf_op jit(solution)/shard_map/reduce_scatter | solution.py:29
  218.0 1.6 add_convert_fusion
  219.6 0.0 all-gather.7.cloned.1.call-update
  219.7 0.2 reduce-scatter.10.cloned.1.call-start
  219.9 0.0 copy-done.4
  219.9 0.2 fusion.4
  220.1 36.4 %all-gather.9.cloned.1.call-done = bf16[8192,256]{1,0:T(8,128)(2,1)} async-done(((bf16[1024,256]{1,0:T(8,128)(2,1)}), bf16[8192,256]{1,0:T(8,128)(2,1)}) %all-gather.9.cloned.1.call-update) | async-done | bytes 4194320 | tf_op jit(solution)/shard_map/all_gather | solution.py:61
  256.5 12.6 %exponential_convert_fusion = bf16[1024,8192]{1,0:T(8,128)(2,1)} fusion(bf16[8192,256]{1,0:T(8,128)(2,1)} %all-gather.9.cloned.1.call-done, bf16[1024,256]{1,0:T(8,128)(2,1)S(1)} %copy-done.4, f32[1024]{0:T(1024)S(1)} %add_rsqrt_fusion.1), kind=kOutput, calls=%fused_computation.5 | convolution fusion | flops 4329308160 | bytes 21499904 | tf_op jit(solution)/shard_map/dot_general | solution.py:62
  269.1 13.2 %all-gather.7.cloned.1.call-done = bf16[64,8192]{1,0:T(8,128)(2,1)} async-done(((bf16[64,1024]{1,0:T(8,128)(2,1)}), bf16[64,8192]{1,0:T(8,128)(2,1)}) %all-gather.7.cloned.1.call-update) | async-done | bytes 1048592 | tf_op jit(solution)/shard_map/all_gather | solution.py:17
  282.3 11.3 %fusion.21 = f32[64,1024]{1,0:T(8,128)S(1)} fusion(bf16[64,8192]{1,0:T(8,128)(2,1)} %all-gather.7.cloned.1.call-done, bf16[1024,8192]{1,0:T(8,128)(2,1)} %exponential_convert_fusion), kind=kOutput, calls=%fused_computation.46 | convolution fusion | flops 1073741824 | bytes 18087936 | tf_op jit(solution)/shard_map/dot_general | solution.py:37
  293.6 24.6 %all-reduce.2 = bf16[64,1024]{1,0:T(8,128)(2,1)S(1)} all-reduce(f32[64,1024]{1,0:T(8,128)S(1)} %fusion.21), channel_id=1, replica_groups=mesh['dp'=8,'tensor'=4] {'tensor'}, use_global_device_ids=true, to_apply=%region_6.7 | all-reduce | flops 65536 | bytes 393216 | tf_op jit(solution)/shard_map/psum | solution.py:65
  318.2 10.1 %convolution_multiply_fusion = f32[64,8192]{1,0:T(8,128)} fusion(bf16[1024,8192]{1,0:T(8,128)(2,1)} %exponential_convert_fusion, bf16[64,1024]{1,0:T(8,128)(2,1)S(1)} %all-reduce.2), kind=kOutput, calls=%fused_computation.6 | convolution fusion | flops 1074266112 | bytes 19005440 | tf_op jit(solution)/shard_map/dot_general | solution.py:33
  328.4 0.0 reduce-scatter.10.cloned.1.call-update
  328.4 0.0 all-gather.11.cloned.1.call-start
  328.4 38.9 %reduce-scatter.10.cloned.1.call-done = f32[64,1024]{1,0:T(8,128)} async-done(((f32[64,8192]{1,0:T(8,128)}), f32[64,1024]{1,0:T(8,128)}) %reduce-scatter.10.cloned.1.call-update) | async-done | bytes 262160 | tf_op jit(solution)/shard_map/reduce_scatter | solution.py:29
  367.3 0.0 copy-start.3
  367.3 1.7 convert_element_type.42
  369.0 0.0 all-gather.11.cloned.1.call-update
  369.0 0.0 copy-start.2
  369.0 0.0 copy-start.5
  369.1 0.3 reduce-scatter.12.cloned.1.call-start
  369.3 24.2 %all-gather.11.cloned.1.call-done = bf16[64,8192]{1,0:T(8,128)(2,1)} async-done(((bf16[64,1024]{1,0:T(8,128)(2,1)}), bf16[64,8192]{1,0:T(8,128)(2,1)}) %all-gather.11.cloned.1.call-update) | async-done | bytes 1048592 | tf_op jit(solution)/shard_map/all_gather | solution.py:17
  393.5 25.9 %fusion.22 = f32[64,4096]{1,0:T(8,128)} fusion(bf16[64,8192]{1,0:T(8,128)(2,1)} %all-gather.11.cloned.1.call-done, bf16[8192,4096]{1,0:T(8,128)(2,1)} %get-tuple-element.20), kind=kOutput, calls=%fused_computation.47 | convolution fusion | flops 4294967296 | bytes 69206016 | tf_op jit(solution)/shard_map/dot_general | solution.py:33
  419.4 0.0 reduce-scatter.12.cloned.1.call-update
  419.4 0.0 reduce-scatter.14.cloned.1.call-start
  419.4 27.2 %reduce-scatter.12.cloned.1.call-done = f32[64,1024]{1,0:T(8,128)} async-done(((f32[64,4096]{1,0:T(8,128)}), f32[64,1024]{1,0:T(8,128)}) %reduce-scatter.12.cloned.1.call-update) | async-done | bytes 262160 | tf_op jit(solution)/shard_map/reduce_scatter | solution.py:21
  446.7 0.0 copy-done.3
  446.7 1.0 fusion.18
  447.7 16.1 %all_gather.23 = bf16[64,4096]{1,0:T(8,128)(2,1)S(1)} all-gather(bf16[64,1024]{1,0:T(8,128)(2,1)S(1)} %get-tuple-element.16), channel_id=1, replica_groups=mesh['dp'=8,'tensor'=4] {'tensor'}, dimensions={1}, use_global_device_ids=true | all-gather | bytes 655360 | tf_op jit(solution)/shard_map/all_gather | solution.py:25
  463.7 30.1 %fusion.23 = f32[64,8192]{1,0:T(8,128)} fusion(bf16[64,4096]{1,0:T(8,128)(2,1)S(1)} %all_gather.23, bf16[8192,4096]{1,0:T(8,128)(2,1)} %get-tuple-element.21), kind=kOutput, calls=%fused_computation.48 | convolution fusion | flops 4294967296 | bytes 69730304 | tf_op jit(solution)/shard_map/dot_general | solution.py:37
  493.9 0.0 reduce-scatter.14.cloned.1.call-update
  493.9 39.6 %reduce-scatter.14.cloned.1.call-done = f32[64,1024]{1,0:T(8,128)} async-done(((f32[64,8192]{1,0:T(8,128)}), f32[64,1024]{1,0:T(8,128)}) %reduce-scatter.14.cloned.1.call-update) | async-done | bytes 262160 | tf_op jit(solution)/shard_map/reduce_scatter | solution.py:29
  533.5 0.0 copy-done.2
  533.5 1.2 multiply_reduce_fusion.1
  534.7 39.4 %all-reduce = (f32[64,1]{0,1:T(1,128)S(1)}, f32[64,1]{0,1:T(1,128)S(1)}, f32[64,1]{0,1:T(1,128)S(1)}, f32[64,1]{0,1:T(1,128)S(1)}) all-reduce(f32[64,1]{0,1:T(1,128)S(1)} %bitcast.25, f32[64,1]{0,1:T(1,128)S(1)} %bitcast.24, f32[64,1]{0,1:T(1,128)S(1)} %bitcast.23, ...), channel_id=1, replica_groups=mesh['dp'=8,'tensor'=4] {'dp','tensor'}, use_global_device_ids=true, to_apply=%region_1.2 | all-reduce | flops 256 | bytes 2048 | tf_op jit(solution)/shard_map/psum | solution.py:72
  574.1 0.0 copy-done.5
  574.1 1.0 multiply_add_fusion
  (7 shorter events, 0.1 us)
Async XLA Ops:
  7.2 67.9 %all-gather.5.cloned.1.call-start = ((), (), s32[]{:S(2)}) async-start(), calls=%async_computation.5 | async-start | bytes 1179648 | tf_op jit(solution)/shard_map/all_gather | solution.py:17
  8.9 122.2 %reduce-scatter.6.cloned.1.call-start = ((), (), s32[]{:S(2)}) async-start(), calls=%async_computation.6 | async-start | bytes 1310720 | tf_op jit(solution)/shard_map/reduce_scatter | solution.py:21
  75.1 56.0 %copy-start = (f32[64,1024]{1,0:T(8,128)S(1)}, f32[64,1024]{1,0:T(8,128)}, u32[]{:S(2)}) copy-start(f32[64,1024]{1,0:T(8,128)} %param.13) | copy-start | bytes 786436
  75.1 56.0 %copy-start.6 = (f32[1024]{0:T(1024)S(1)}, f32[1024]{0:T(1024)}, u32[]{:S(2)}) copy-start(f32[1024]{0:T(1024)} %param.10) | copy-start | bytes 12292
  75.1 103.2 %copy-start.1 = (bf16[1024,256]{1,0:T(8,128)(2,1)S(1)}, bf16[1024,256]{1,0:T(8,128)(2,1)}, u32[]{:S(2)}) copy-start(bf16[1024,256]{1,0:T(8,128)(2,1)} %param.8) | copy-start | bytes 1572868
  75.1 144.8 %copy-start.4 = (bf16[1024,256]{1,0:T(8,128)(2,1)S(1)}, bf16[1024,256]{1,0:T(8,128)(2,1)}, u32[]{:S(2)}) copy-start(bf16[1024,256]{1,0:T(8,128)(2,1)} %param.7) | copy-start | bytes 1572868
  101.0 117.0 %reduce-scatter.8.cloned.1.call-start = ((), (), s32[]{:S(2)}) async-start(), calls=%async_computation.7 | async-start | bytes 2359296 | tf_op jit(solution)/shard_map/reduce_scatter | solution.py:29
  178.2 78.3 %all-gather.9.cloned.1.call-start = ((), (), s32[]{:S(2)}) async-start(), calls=%async_computation.9 | async-start | bytes 4718592 | tf_op jit(solution)/shard_map/all_gather | solution.py:61
  179.5 102.8 %all-gather.7.cloned.1.call-start = ((), (), s32[]{:S(2)}) async-start(), calls=%async_computation.8 | async-start | bytes 1179648 | tf_op jit(solution)/shard_map/all_gather | solution.py:17
  219.7 147.6 %reduce-scatter.10.cloned.1.call-start = ((), (), s32[]{:S(2)}) async-start(), calls=%async_computation.10 | async-start | bytes 2359296 | tf_op jit(solution)/shard_map/reduce_scatter | solution.py:29
  328.4 65.1 %all-gather.11.cloned.1.call-start = ((), (), s32[]{:S(2)}) async-start(), calls=%async_computation.11 | async-start | bytes 1179648 | tf_op jit(solution)/shard_map/all_gather | solution.py:17
  367.3 79.4 %copy-start.3 = (f32[64,1024]{1,0:T(8,128)S(1)}, f32[64,1024]{1,0:T(8,128)}, u32[]{:S(2)}) copy-start(f32[64,1024]{1,0:T(8,128)} %reduce-scatter.10.cloned.1.call-done) | copy-start | bytes 786436
  369.0 164.5 %copy-start.2 = (f32[64,1024]{1,0:T(8,128)S(1)}, f32[64,1024]{1,0:T(8,128)}, u32[]{:S(2)}) copy-start(f32[64,1024]{1,0:T(8,128)} %param.12) | copy-start | bytes 786436
  369.0 205.0 %copy-start.5 = (f32[64,1024]{1,0:T(8,128)S(1)}, f32[64,1024]{1,0:T(8,128)}, u32[]{:S(2)}) copy-start(f32[64,1024]{1,0:T(8,128)} %param.11) | copy-start | bytes 786436
  369.1 77.6 %reduce-scatter.12.cloned.1.call-start = ((), (), s32[]{:S(2)}) async-start(), calls=%async_computation.12 | async-start | bytes 1310720 | tf_op jit(solution)/shard_map/reduce_scatter | solution.py:21
  419.4 114.1 %reduce-scatter.14.cloned.1.call-start = ((), (), s32[]{:S(2)}) async-start(), calls=%async_computation.13 | async-start | bytes 2359296 | tf_op jit(solution)/shard_map/reduce_scatter | solution.py:29
Sparse Core Ops, SparseCore 0:
  10.5 26.1 all-gather.4
  101.1 29.8 reduce-scatter.5
  178.3 39.6 reduce-scatter.7
  219.8 36.6 all-gather.8
  258.8 23.4 all-gather.6
  328.5 38.7 reduce-scatter.9
  370.0 23.4 all-gather.10
  419.5 27.1 reduce-scatter.11
  494.0 39.4 reduce-scatter.13
where the time goes:
time: 582 us
  waiting for transfers between devices  248 us (43%)
  matrix products  146 us (25%)
  blocking collectives  96 us (16%)
  other arithmetic  76.7 us (13%)
  between operations  14 us (2%)
    reduce_scatter x3, waiting for transfers between devices, rows_out(): lax.psum_scatter(partial_value, 'dp', scatter_dimension=1, tiled=True)  117 us
    dot_general x3, matrix products, times_block_t(): lax.dot_general(vector_cols, block, (((1,), (1,)), ((), ())), preferred_e...  71.6 us
    select_n x1, other arithmetic, shards(): upper = jnp.where(col_ids >= row_ids, factors, zero_block)  66.1 us
    dot_general x3, matrix products, times_block(): return jnp.dot(vector_rows, block, preferred_element_type=jnp.float32)  61.9 us
    reduce_scatter x2, waiting for transfers between devices, cols_out(): lax.psum_scatter(partial_value, 'tensor', scatter_dimension=1, tiled=True)  57.2 us
    psum x1, blocking collectives, shards(): lax.psum((jnp.sum(residual * residual, axis=1, keepdims=True), jnp.sum(di...  39.4 us
    all_gather x3, waiting for transfers between devices, rows_in(): return lax.all_gather(vector_b, 'dp', axis=1, tiled=True)  37.4 us
    all_gather x1, waiting for transfers between devices, shards(): center_rows = lax.all_gather(normalized(centers), 'dp', axis=0, tiled=True)  36.4 us
  transfers between devices with their start and end apart: 9, of which 8 were waited for; matrix products, arithmetic and copies ran while one was open for 14% of the time, Pallas kernels for 0%

commit v1 on v0

--- a/solution.py
+++ b/solution.py
@@ -1,6 +1,10 @@
+import functools
+
 import jax
 import jax.numpy as jnp
 from jax import lax
+from jax.experimental import pallas as pl
+from jax.experimental.pallas import tpu as pltpu
 from jax.sharding import PartitionSpec as P
 
 kernel_gamma = 8.0
@@ -37,6 +41,514 @@
     return lax.dot_general(
         vector_cols, block, (((1,), (1,)), ((), ())), preferred_element_type=jnp.float32
     )
+
+
+MESH = pl.DeviceIdType.MESH
+SLOTS = 3
+F32 = jnp.float32
+BF16 = jnp.bfloat16
+
+
+def dot_nn(a, b):
+    return jnp.dot(a, b, preferred_element_type=F32)
+
+
+def dot_nt(a, b):
+    return lax.dot_general(a, b, (((1,), (1,)), ((), ())), preferred_element_type=F32)
+
+
+def fused(
+    nd,
+    nt,
+    points,
+    centers,
+    factors,
+    scale,
+    iterate,
+    residual,
+    direction,
+    new_iterate,
+    new_residual,
+    new_direction,
+    fbuf,
+    kmat,
+    xn,
+    cen,
+    rows,
+    acc,
+    own,
+    first,
+    zsend,
+    zrecv,
+    zgath,
+    rsend,
+    rrecv,
+    psend,
+    precv,
+    pgath,
+    stat_dp,
+    stat_t,
+    fsem,
+    ag_s,
+    ag_r,
+    cag_s,
+    cag_r,
+    zr_s,
+    zr_r,
+    zg_s,
+    zg_r,
+    rs_s,
+    rs_r,
+    pr_s,
+    pr_r,
+    pg_s,
+    pg_r,
+    sd_s,
+    sd_r,
+    st_s,
+    st_r,
+):
+    d = lax.axis_index("dp")
+    t = lax.axis_index("tensor")
+    piece = direction.shape[1]
+    pts = points.shape[0]
+    width = pts // nt
+    core = lax.rem(d, 2)
+    chip = lax.div(d, 2)
+    nchip = nd // 2
+    sib = d + 1 - 2 * core
+
+    def dp_at(m):
+        return lax.rem(d + m, nd)
+
+    def t_at(m):
+        return lax.rem(t + m, nt)
+
+    def send(src, dst, ssem, rsem, dp, tp):
+        return pltpu.make_async_remote_copy(
+            src_ref=src,
+            dst_ref=dst,
+            send_sem=ssem,
+            recv_sem=rsem,
+            device_id=(dp, tp),
+            device_id_type=MESH,
+        )
+
+    def load(q):
+        slot = lax.rem(q, SLOTS)
+        return pltpu.make_async_copy(
+            factors.at[pl.ds(pl.multiple_of(q * piece, piece), piece), :],
+            fbuf.at[slot],
+            fsem.at[slot],
+        )
+
+    for q in range(SLOTS):
+        load(jnp.int32(nd - 1 - q)).start()
+
+    barrier = pltpu.get_barrier_semaphore()
+    for m in range(1, nd):
+        pl.semaphore_signal(barrier, inc=1, device_id=(dp_at(m), t), device_id_type=MESH)
+    for m in range(1, nt):
+        pl.semaphore_signal(barrier, inc=1, device_id=(d, t_at(m)), device_id_type=MESH)
+
+    def normal(x):
+        wide = x.astype(F32)
+        inv = lax.rsqrt(jnp.mean(wide * wide, axis=1, keepdims=True) + 1e-06)
+        return (wide * inv).astype(BF16)
+
+    rows[0, d] = direction[...].astype(BF16)
+    cen[d] = normal(centers[...])
+    pl.semaphore_wait(barrier, nd - 1 + nt - 1)
+
+    def out_copy(buf, ss, rs, m):
+        if m == 0:
+            return send(buf.at[d], buf.at[d], ss.at[0], rs.at[d], sib, t)
+        to = lax.rem(chip + m, nchip) * 2 + core
+        return send(buf.at[d], buf.at[d], ss.at[m], rs.at[d], to, t)
+
+    def on_copy(buf, ss, rs, m):
+        src = lax.rem(chip - m + nchip, nchip) * 2 + core
+        return send(buf.at[src], buf.at[src], ss.at[nchip + m - 1], rs.at[src], sib, t)
+
+    def ag_start(buf, ss, rs):
+        for m in range(nchip):
+            out_copy(buf, ss, rs, m).start()
+
+    def ag_forward(buf, ss, rs):
+        for m in range(1, nchip):
+            c = on_copy(buf, ss, rs, m)
+            c.wait_recv()
+            c.start()
+
+    def ag_finish(buf, ss, rs):
+        for m in range(nchip):
+            src = m * 2 + 1 - core
+            send(buf.at[src], buf.at[src], ss.at[0], rs.at[src], sib, t).wait_recv()
+        for m in range(nchip):
+            out_copy(buf, ss, rs, m).wait_send()
+        for m in range(1, nchip):
+            on_copy(buf, ss, rs, m).wait_send()
+
+    ag_start(rows.at[0], ag_s.at[0], ag_r.at[0])
+    ag_start(cen, cag_s, cag_r)
+    xn[...] = normal(points[...])
+    ag_forward(rows.at[0], ag_s.at[0], ag_r.at[0])
+    ag_finish(rows.at[0], ag_s.at[0], ag_r.at[0])
+
+    def tile(q, j):
+        return fbuf[lax.rem(q, SLOTS), :, pl.ds(pl.multiple_of(j * piece, piece), piece)]
+
+    def masked(q, upper):
+        block = tile(q, t)
+        row = lax.broadcasted_iota(jnp.int32, (piece, piece), 0)
+        col = lax.broadcasted_iota(jnp.int32, (piece, piece), 1)
+        keep = col >= row if upper else col < row
+        return jnp.where(keep, block, jnp.zeros_like(block))
+
+    def times_rows(q, x, lo, hi):
+        def step(j, carry):
+            acc[j] += dot_nn(x, tile(q, j))
+            return carry
+
+        lax.fori_loop(lo, hi, step, 0)
+
+    def times_cols(q, phase, lo, hi):
+        def step(j, carry):
+            own[...] += dot_nt(zgath[phase, j], tile(q, j))
+            return carry
+
+        lax.fori_loop(lo, hi, step, 0)
+
+    def rs_copy(phase, q):
+        return send(
+            rsend.at[q], rrecv.at[phase, d], rs_s.at[phase, q], rs_r.at[phase, d], q, t
+        )
+
+    def rs_wait(phase, src):
+        send(
+            rsend.at[src], rrecv.at[phase, src], rs_s.at[phase, src], rs_r.at[phase, src], src, t
+        ).wait_recv()
+
+    def exchange(phase, finish):
+        for m in range(1, nt):
+            j = t_at(m)
+            zsend[j] = acc[j].astype(BF16)
+            send(
+                zsend.at[j], zrecv.at[phase, t], zr_s.at[phase, j], zr_r.at[phase, t], d, j
+            ).start()
+        total = acc[t]
+        for m in range(1, nt):
+            j = t_at(m)
+            send(
+                zsend.at[j], zrecv.at[phase, j], zr_s.at[phase, j], zr_r.at[phase, j], d, j
+            ).wait_recv()
+            total = total + zrecv[phase, j].astype(F32)
+        zgath[phase, t] = finish(total).astype(BF16)
+        for m in range(1, nt):
+            j = t_at(m)
+            send(
+                zgath.at[phase, t], zgath.at[phase, t], zg_s.at[phase, j], zg_r.at[phase, t], d, j
+            ).start()
+        for m in range(1, nt):
+            j = t_at(m)
+            send(
+                zgath.at[phase, j], zgath.at[phase, j], zg_s.at[phase, j], zg_r.at[phase, j], d, j
+            ).wait_recv()
+        for m in range(1, nt):
+            j = t_at(m)
+            send(
+                zsend.at[j], zrecv.at[phase, t], zr_s.at[phase, j], zr_r.at[phase, t], d, j
+            ).wait_send()
+            send(
+                zgath.at[phase, t], zgath.at[phase, t], zg_s.at[phase, j], zg_r.at[phase, t], d, j
+            ).wait_send()
+
+    def factor_phase(phase, upper, finish):
+        slab = rows.at[0 if phase == 0 else 2]
+        down = not upper
+        before = nd - 1 - d if down else d
+        after = d if down else nd - 1 - d
+
+        def nth(i):
+            return nd - 1 - i if down else i
+
+        def ready(i):
+            if down:
+                load(nth(i)).wait()
+            else:
+
+                @pl.when(i >= SLOTS)
+                def _():
+                    load(nth(i)).wait()
+
+        def done(i):
+            @pl.when(i + SLOTS < nd)
+            def _():
+                load(nth(i + SLOTS)).start()
+
+        acc[...] = jnp.zeros_like(acc)
+
+        def first_half(i, carry):
+            ready(i)
+            q = nth(i)
+            times_rows(q, slab[q], 0, nt)
+            done(i)
+            return carry
+
+        lax.fori_loop(0, before, first_half, 0)
+        ready(before)
+        x = slab[d]
+        if upper:
+            times_rows(d, x, t + 1, nt)
+        else:
+            times_rows(d, x, 0, t)
+        acc[t] += dot_nn(x, masked(d, upper))
+        exchange(phase, finish)
+
+        def second_half(i, carry):
+            ready(i)
+            q = nth(i)
+            own[...] = jnp.zeros_like(own)
+            times_cols(q, phase, 0, nt)
+            rsend[q] = own[...].astype(BF16)
+            rs_copy(2 * phase, q).start()
+            done(i)
+            return carry
+
+        own[...] = dot_nt(zgath[phase, t], masked(d, not upper))
+        if upper:
+            times_cols(d, phase, 0, t)
+        else:
+            times_cols(d, phase, t + 1, nt)
+        done(before)
+        kept = own[...]
+        lax.fori_loop(before + 1, nd, second_half, 0)
+        return kept
+
+    def factor_sum(phase, upper, total):
+        lo, hi = (0, d) if upper else (d + 1, nd)
+        slo, shi = (d + 1, nd) if upper else (0, d)
+        own[...] = total
+
+        def got(src, carry):
+            rs_wait(2 * phase, src)
+            own[...] += rrecv[2 * phase, src].astype(F32)
+            return carry
+
+        lax.fori_loop(lo, hi, got, 0)
+
+        def gone(q, carry):
+            rs_copy(2 * phase, q).wait_send()
+            return carry
+
+        lax.fori_loop(slo, shi, gone, 0)
+        return own[...]
+
+    def form(lo, hi):
+        def step(i, carry):
+            q = lax.div(i, 4)
+            at = pl.ds(pl.multiple_of(lax.rem(i, 4) * (pts // 4), pts // 4), pts // 4)
+            inner = dot_nt(xn[at, :], cen[q])
+            kmat[q, at, :] = jnp.exp(
+                kernel_gamma * (inner / points.shape[1] - 1.0)
+            ).astype(BF16)
+            return carry
+
+        lax.fori_loop(4 * lo, 4 * hi, step, 0)
+
+    def finish_first(total):
+        first[...] = scale[...] * (direction[...] + total)
+        return first[...]
+
+    kept = factor_phase(0, False, finish_first)
+    ag_forward(cen, cag_s, cag_r)
+    ag_finish(cen, cag_s, cag_r)
+    acc[0] = kept
+    form(0, nd // 2)
+    second = factor_sum(0, False, first[...] + acc[0])
+    rows[1, d] = second.astype(BF16)
+    ag_start(rows.at[1], ag_s.at[1], ag_r.at[1])
+    form(nd // 2, nd)
+    ag_forward(rows.at[1], ag_s.at[1], ag_r.at[1])
+    ag_finish(rows.at[1], ag_s.at[1], ag_r.at[1])
+
+    own[:, :pts] = jnp.zeros((own.shape[0], pts), F32)
+
+    def to_points(q, carry):
+        own[:, :pts] += dot_nt(rows[1, q], kmat[q])
+        return carry
+
+    lax.fori_loop(0, nd, to_points, 0)
+    for j in range(nt):
+        acc[j, :, :width] = own[:, j * width : (j + 1) * width]
+        psend[j] = own[:, j * width : (j + 1) * width].astype(BF16)
+    for m in range(1, nt):
+        j = t_at(m)
+        send(psend.at[j], precv.at[t], pr_s.at[j], pr_r.at[t], d, j).start()
+    total = acc[t, :, :width]
+    for m in range(1, nt):
+        j = t_at(m)
+        send(psend.at[j], precv.at[j], pr_s.at[j], pr_r.at[j], d, j).wait_recv()
+        total = total + precv[j].astype(F32)
+    pgath[t] = total.astype(BF16)
+    for m in range(1, nt):
+        j = t_at(m)
+        send(pgath.at[t], pgath.at[t], pg_s.at[j], pg_r.at[t], d, j).start()
+    for m in range(1, nt):
+        j = t_at(m)
+        send(pgath.at[j], pgath.at[j], pg_s.at[j], pg_r.at[j], d, j).wait_recv()
+    for m in range(1, nt):
+        j = t_at(m)
+        send(psend.at[j], precv.at[t], pr_s.at[j], pr_r.at[t], d, j).wait_send()
+        send(pgath.at[t], pgath.at[t], pg_s.at[j], pg_r.at[t], d, j).wait_send()
+
+    def from_points(q):
+        part = dot_nn(pgath[0], kmat[q, :width, :])
+        for j in range(1, nt):
+            part += dot_nn(pgath[j], kmat[q, j * width : (j + 1) * width, :])
+        return part / (pts * nd)
+
+    def back_step(m, carry):
+        q = lax.rem(d + m, nd)
+        rsend[q] = from_points(q).astype(BF16)
+        rs_copy(1, q).start()
+        return carry
+
+    lax.fori_loop(1, nd, back_step, 0)
+    own[...] = from_points(d)
+
+    def back_sum(m, carry):
+        src = lax.rem(d + nd - m, nd)
+        rs_wait(1, src)
+        own[...] += rrecv[1, src].astype(F32)
+        return carry
+
+    lax.fori_loop(1, nd, back_sum, 0)
+
+    def back_gone(m, carry):
+        rs_copy(1, lax.rem(d + m, nd)).wait_send()
+        return carry
+
+    lax.fori_loop(1, nd, back_gone, 0)
+    back = own[...]
+    rows[2, d] = back.astype(BF16)
+    ag_start(rows.at[2], ag_s.at[2], ag_r.at[2])
+    first[...] = back + ridge_penalty * first[...]
+    ag_forward(rows.at[2], ag_s.at[2], ag_r.at[2])
+    ag_finish(rows.at[2], ag_s.at[2], ag_r.at[2])
+
+    def finish_weighted(total):
+        first[...] = scale[...] * (first[...] + total)
+        return first[...]
+
+    kept = factor_phase(1, True, finish_weighted)
+    image = factor_sum(1, True, first[...] + kept)
+    r = residual[...]
+    p = direction[...]
+    lane = lax.broadcasted_iota(jnp.int32, (r.shape[0], 128), 1)
+
+    def summed(v):
+        return jnp.sum(v, axis=1, keepdims=True)
+
+    stat = jnp.where(lane == 0, summed(r * r), 0.0)
+    stat = jnp.where(lane == 1, summed(p * image), stat)
+    stat = jnp.where(lane == 2, summed(r * image), stat)
+    stat = jnp.where(lane == 3, summed(image * image), stat)
+    stat_dp[d] = stat
+
+    def stat_copy(m):
+        q = dp_at(m)
+        return send(stat_dp.at[d], stat_dp.at[d], sd_s.at[q], sd_r.at[d], q, t)
+
+    for m in range(1, nd):
+        stat_copy(m).start()
+    for m in range(1, nd):
+        q = dp_at(m)
+        send(stat_dp.at[q], stat_dp.at[q], sd_s.at[q], sd_r.at[q], q, t).wait_recv()
+    stat = stat_dp[0]
+    for q in range(1, nd):
+        stat = stat + stat_dp[q]
+    stat_t[t] = stat
+    for m in range(1, nt):
+        j = t_at(m)
+        send(stat_t.at[t], stat_t.at[t], st_s.at[j], st_r.at[t], d, j).start()
+    for m in range(1, nt):
+        j = t_at(m)
+        send(stat_t.at[j], stat_t.at[j], st_s.at[j], st_r.at[j], d, j).wait_recv()
+    for m in range(1, nt):
+        j = t_at(m)
+        send(stat_t.at[t], stat_t.at[t], st_s.at[j], st_r.at[t], d, j).wait_send()
+    for m in range(1, nd):
+        stat_copy(m).wait_send()
+    stat = stat_t[0]
+    for j in range(1, nt):
+        stat = stat + stat_t[j]
+    old_norm, curvature = stat[:, 0:1], stat[:, 1:2]
+    cross, image_norm = stat[:, 2:3], stat[:, 3:4]
+    step_size = old_norm / curvature
+    new_iterate[...] = iterate[...] + step_size * p
+    image = own[...]
+    nr = r - step_size * image
+    new_residual[...] = nr
+    new_norm = old_norm - 2.0 * step_size * cross + step_size * step_size * image_norm
+    new_direction[...] = nr + new_norm / old_norm * p
+
+
+def fused_shards(nd, nt, points, centers, factors, column_scale, iterate, residual, direction):
+    r, piece = direction.shape
+    pts, dim = points.shape
+    local_cols = factors.shape[1]
+    width = pts // nt
+    vmem = pl.BlockSpec(memory_space=pltpu.VMEM)
+    dma = pltpu.SemaphoreType.DMA
+    return pl.pallas_call(
+        functools.partial(fused, nd, nt),
+        out_shape=(jax.ShapeDtypeStruct((r, piece), F32),) * 3,
+        in_specs=[vmem, vmem, pl.BlockSpec(memory_space=pl.ANY), vmem, vmem, vmem, vmem],
+        out_specs=(vmem, vmem, vmem),
+        scratch_shapes=[
+            pltpu.VMEM((SLOTS, piece, local_cols), BF16),
+            pltpu.VMEM((nd, pts, piece), BF16),
+            pltpu.VMEM((pts, dim), BF16),
+            pltpu.VMEM((nd, piece, dim), BF16),
+            pltpu.VMEM((3, nd, r, piece), BF16),
+            pltpu.VMEM((nt, r, piece), F32),
+            pltpu.VMEM((r, piece), F32),
+            pltpu.VMEM((r, piece), F32),
+            pltpu.VMEM((nt, r, piece), BF16),
+            pltpu.VMEM((2, nt, r, piece), BF16),
+            pltpu.VMEM((2, nt, r, piece), BF16),
+            pltpu.VMEM((nd, r, piece), BF16),
+            pltpu.VMEM((3, nd, r, piece), BF16),
+            pltpu.VMEM((nt, r, width), BF16),
+            pltpu.VMEM((nt, r, width), BF16),
+            pltpu.VMEM((nt, r, width), BF16),
+            pltpu.VMEM((nd, r, 128), F32),
+            pltpu.VMEM((nt, r, 128), F32),
+            dma((SLOTS,)),
+            dma((3, nd)),
+            dma((3, nd)),
+            dma((nd,)),
+            dma((nd,)),
+            dma((2, nt)),
+            dma((2, nt)),
+            dma((2, nt)),
+            dma((2, nt)),
+            dma((3, nd)),
+            dma((3, nd)),
+            dma((nt,)),
+            dma((nt,)),
+            dma((nt,)),
+            dma((nt,)),
+            dma((nd,)),
+            dma((nd,)),
+            dma((nt,)),
+            dma((nt,)),
+        ],
+        compiler_params=pltpu.CompilerParams(
+            collective_id=0, has_side_effects=True, vmem_limit_bytes=63 * 1024 * 1024
+        ),
+    )(points, centers, factors, column_scale[None, :], iterate, residual, direction)
 
 
 def shards(points, centers, factors, column_scale, iterate, residual, direction):
@@ -87,8 +599,19 @@
 
 
 def solution(mesh):
+    nd, nt = mesh.shape["dp"], mesh.shape["tensor"]
+
+    def local(points, centers, factors, *vectors):
+        piece = vectors[-1].shape[1]
+        pts = points.shape[0]
+        vmem = 2 * (3 * piece * factors.shape[1] + nd * pts * piece)
+        whole_tiles = piece % 128 == 0 and pts % (128 * nt) == 0 and pts <= piece
+        if whole_tiles and nd % 2 == 0 and nd > SLOTS and vmem <= 42 * 1024 * 1024:
+            return fused_shards(nd, nt, points, centers, factors, *vectors)
+        return shards(points, centers, factors, *vectors)
+
     return jax.shard_map(
-        shards,
+        local,
         mesh=mesh,
         in_specs=(
             P("dp", None),

time: 582 us -> 196 us (0.34)
  waiting for transfers between devices: 248 us -> 0 us
  Pallas kernels: 0 us -> 190 us
  matrix products: 146 us -> 0 us
  blocking collectives: 96 us -> 0 us
  other arithmetic: 76.7 us -> 0 us
  between operations: 14 us -> 0.64 us
    pallas_call x0 -> x1, Pallas kernels: none -> 190 us  [fused_shards(): pl.pallas_call(functools.partial(fused, nd, nt), out_shape=(jax.ShapeDtyp...]
    reduce_scatter x5 -> x0, waiting for transfers between devices: 174 us -> none  [the longest x3 117 us: rows_out(): lax.psum_scatter(partial_value, 'dp', scatter_dimension=1, tiled=True)]
    dot_general x7 -> x0, matrix products: 146 us -> none  [the longest x3 71.6 us: times_block_t(): lax.dot_general(vector_cols, block, (((1,), (1,)), ((), ())), preferred_e...]
    all_gather x4 -> x0, waiting for transfers between devices: 73.8 us -> none  [the longest x3 37.4 us: rows_in(): return lax.all_gather(vector_b, 'dp', axis=1, tiled=True)]
    select_n x1 -> x0, other arithmetic: 66.1 us -> none  [shards(): upper = jnp.where(col_ids >= row_ids, factors, zero_block)]
    psum x2 -> x0, blocking collectives: 63.9 us -> none  [the longest x1 39.4 us: shards(): lax.psum((jnp.sum(residual * residual, axis=1, keepdims=True), jnp.sum(di...]
    all_gather x2 -> x0, blocking collectives: 32.1 us -> none  [cols_in(): return lax.all_gather(vector_b, 'tensor', axis=1, tiled=True)]
    convert_element_type x6 -> x0, other arithmetic: 7.93 us -> none  [the longest x1 1.69 us: shards(): back_b_rows = rows_in(back.astype(jnp.bfloat16))]
  transfers between devices with their start and end apart: 9 -> 0, of which waited for: 8 -> 0; matrix products, arithmetic and copies ran while one was open for 14% -> 0% of each run, Pallas kernels for 0% -> 0%
where the time goes in v1:
time: 196 us; the launch traced here: 195 us
  Pallas kernels  190 us (97%)
  local copies, waits for them, and re-layouts  5.01 us (3%)
    pallas_call x1, Pallas kernels, fused_shards(): pl.pallas_call(functools.partial(fused, nd, nt), out_shape=(jax.ShapeDtyp...  190 us
    unnamed x3, local copies, waits for them, and re-layouts  5.01 us

profile of v1, /device:TPU:0, one launch (start us, length us, event | category | flops | bytes accessed | tf_op | source)
XLA Modules:
  0.0 195.5 jit_solution(16077731596810799159)
XLA Ops:
  0.6 189.8 %shard_map.94 = (f32[64,1024]{1,0:T(8,128)}, f32[64,1024]{1,0:T(8,128)}, f32[64,1024]{1,0:T(8,128)}) custom-call(bf16[1024,256]{1,0:T(8,128)(2,1)} %points.1, bf16[1024,256]{1,0:T(8,128)(2,1)} %centers.1, bf16[8192,4096]{1,0:T(8,128)(2,1)} %factors.1, f32[1,1024]{1,0:T(1,128)} %bitcast.1, f32[64,1024]{1,0:T(8,128)} %iterate.1, f32[64,1024]{1,0:T(8,128)} %residual.1, ...), custom_call_target="tpu_custom_call" | custom-call | tf_op jit(solution)/shard_map/pallas_call | solution.py:504
  190.5 1.7 copy.13
  192.1 1.7 copy.14
  193.8 1.7 copy.15
